TPU v7x, 128 devices: a whole 4x4x4 slice. The times are simulated.
128 devices in a mesh: seq: 32 (over y, x, core), head: 4 (over z).
Axes of the slice: x: 4, y: 4, z: 4, core: 2. Of those that a mesh axis runs over, the one named last changes fastest.
Arguments:
- tokens: bfloat16 [32768, 768], P('seq'), may hold values from -6 to 6
- cluster_of: int32 [32768], P('seq'), may hold values from 0 to 127, as said below
- w_query: bfloat16 [3, 768, 768], P(None, 'head')
- w_key: bfloat16 [3, 768, 768], P(None, 'head')
- w_value: bfloat16 [3, 768, 768], P(None, 'head'), may hold values from -0.21875 to 0.21875
- w_out: bfloat16 [3, 768, 768], replicated, may hold values from -0.21875 to 0.21875
Outputs:
- mixed: bfloat16 [32768, 768], P('seq')
Inputs may be any that keep to these rules, and one draw needn't show every extreme that they name: `cluster_of`: owner k holds the 4 clusters k * 4 to (k + 1) * 4 - 1. Of the 1024 tokens of one device, at most 64 lie in one owner's clusters, and in every draw one owner has exactly 64 tokens from every device.
All inputs are finite; a program needn't handle non-finite values.
Results may differ from a plain program's by a relative error of at most 0.012.
Values may be sent and summed in bfloat16 or wider, within the bound.
A program may use at most 128 MiB of HBM per device.

v0:
```python
import math
import types

import jax
import jax.numpy as jnp
from jax import lax
from jax.experimental import pallas as pl
from jax.experimental.pallas import tpu as pltpu
from jax.sharding import PartitionSpec as P

MESH = pl.DeviceIdType.MESH
D = 768
ROWS = 1024
HALF = 128
NS = 32
NH = 4
SLOTS = 64
PAIR = 256
NPAIR = ROWS // PAIR
LAST = NH - 1
FAR = -1e30
Q_SCALE = math.log2(math.e) / 8.0
VMEM_LIMIT = 60 * 1024 * 1024

NT = (((1,), (1,)), ((), ()))
NN = (((1,), (0,)), ((), ()))


def matmul(a, b, dims=NN):
    return lax.dot_general(a, b, dims, preferred_element_type=jnp.float32)


def lanes(shape):
    return lax.broadcasted_iota(jnp.int32, shape, 1)


def row_normed(rows):
    wide = rows.astype(jnp.float32)
    factor = lax.rsqrt(jnp.mean(wide * wide, axis=1, keepdims=True) + 1e-05)
    return (wide * factor).astype(jnp.bfloat16)


def only_head(rows, h):
    lane = lanes(rows.shape)
    keep = ((lane >= 64 * h) & (lane < 64 * h + 64)) | (lane >= 192)
    return jnp.where(keep, rows, jnp.zeros_like(rows))


def half_turn(rows):
    return pltpu.roll(rows, 64, 1)


def packed_third(third):
    m = third.shape[0] // 2
    return jnp.where(lanes((m, 128)) < 64, half_turn(third[:m]), third[m:])


GROUP = 4
NGROUP = NS // GROUP
GROWS = GROUP * SLOTS
ANSWER = SLOTS + SLOTS // 2
PACKED = PAIR + PAIR // 2

BF16, F32 = jnp.bfloat16, jnp.float32
DMA = pltpu.SemaphoreType.DMA
SCRATCH = {
    "x0": pltpu.VMEM((ROWS, D), BF16),
    "x1": pltpu.VMEM((ROWS, D), BF16),
    "x2": pltpu.VMEM((PAIR, D), BF16),
    "x3": pltpu.VMEM((ROWS, D), BF16),
    "w0": pltpu.VMEM((768, D), BF16),
    "w1": pltpu.VMEM((640, D), BF16),
    "w2": pltpu.VMEM((NH, 768, D), BF16),
    "wo": pltpu.VMEM((3, 768, D), BF16),
    "halo0": pltpu.VMEM((2, HALF, D), BF16),
    "halo2": pltpu.VMEM((2, HALF, D), BF16),
    "q0": pltpu.VMEM((ROWS, 256), BF16),
    "k0": pltpu.VMEM((ROWS + 2 * HALF, 256), BF16),
    "v0": pltpu.VMEM((ROWS + 2 * HALF, 256), BF16),
    "q2": pltpu.VMEM((NH, PAIR, 256), BF16),
    "k2": pltpu.VMEM((NH, PAIR + 2 * HALF, 256), BF16),
    "v2": pltpu.VMEM((NH, PAIR + 2 * HALF, 256), BF16),
    "att0": pltpu.VMEM((NH, NPAIR, PACKED, 128), BF16),
    "att1": pltpu.VMEM((NH, PACKED, 128), BF16),
    "own1": pltpu.VMEM((NPAIR, PACKED, 128), BF16),
    "chosen": pltpu.VMEM((NS * SLOTS, ROWS), BF16),
    "chosen_back": pltpu.VMEM((ROWS, NS * SLOTS), BF16),
    "within": pltpu.VMEM((ROWS, 128), F32),
    "packed": pltpu.VMEM((ROWS, 640), BF16),
    "out_kv": pltpu.VMEM((NS, SLOTS, 512), BF16),
    "out_q": pltpu.VMEM((NS, SLOTS, 128), BF16),
    "in_kv": pltpu.VMEM((NS, SLOTS, 512), BF16),
    "in_q": pltpu.VMEM((NS, SLOTS, 128), BF16),
    "k_all": pltpu.VMEM((NS * SLOTS, 256), BF16),
    "v_all": pltpu.VMEM((NS * SLOTS, 256), BF16),
    "answer": pltpu.VMEM((NS, ANSWER, 128), BF16),
    "back": pltpu.VMEM((NS, ANSWER, 128), BF16),
    "back_all": pltpu.VMEM((NS * SLOTS, 256), BF16),
    "x_sems": DMA((NPAIR,)),
    "w0_sems": DMA((4,)),
    "w1_sems": DMA((5,)),
    "w2_sems": DMA((4,)),
    "w2_send": DMA((NH, 4)),
    "w2_recv": DMA((NH, 4)),
    "wo_sems": DMA((3, 2 * NH)),
    "halo0_send": DMA((2,)),
    "halo0_recv": DMA((2,)),
    "halo2_send": DMA((2,)),
    "halo2_recv": DMA((2,)),
    "att0_send": DMA((NPAIR, NH)),
    "att0_recv": DMA((NPAIR, NH)),
    "att1_send": DMA((NH,)),
    "att1_recv": DMA((NH,)),
    "kv_send": DMA((NS,)),
    "kv_recv": DMA((NS,)),
    "q_send": DMA((NS,)),
    "q_recv": DMA((NS,)),
    "a_send": DMA((NS,)),
    "a_recv": DMA((NS,)),
    "x3_send": DMA((2, NH)),
    "x3_recv": DMA((2, NH)),
    "out_sems": DMA((2, NH)),
}
N_ARGS = 7


def remote(src, dst, send_sem, recv_sem, device):
    return pltpu.make_async_remote_copy(
        src_ref=src,
        dst_ref=dst,
        send_sem=send_sem,
        recv_sem=recv_sem,
        device_id=device,
        device_id_type=MESH,
    )


def window_loads(source, target, sems):
    wq, wk, wv = source
    return [
        pltpu.make_async_copy(wq, target.at[pl.ds(0, 192)], sems.at[0]),
        pltpu.make_async_copy(wk, target.at[pl.ds(256, 192)], sems.at[1]),
        pltpu.make_async_copy(wv.at[pl.ds(0, 128)], target.at[pl.ds(512, 128)], sems.at[2]),
        pltpu.make_async_copy(wv.at[pl.ds(128, 64)], target.at[pl.ds(704, 64)], sems.at[3]),
    ]


def keep_keys(projected, k_rows, v_rows):
    k_rows[...] = projected[:, 0:256].astype(BF16)
    lane = lanes((projected.shape[0], 256))
    ones = (lane >= 128) & (lane < 192)
    v_rows[...] = jnp.where(ones, 1.0, projected[:, 256:512]).astype(BF16)


def window_block(queries, keys, values, place):
    query = lax.broadcasted_iota(jnp.int32, (HALF, 3 * HALF), 0)
    key = lax.broadcasted_iota(jnp.int32, (HALF, 3 * HALF), 1)
    allowed = (
        (key >= query)
        & (key < query + 2 * HALF)
        & (place + key >= 0)
        & (place + key < NS * ROWS)
    )
    bias = jnp.where(allowed, 0.0, FAR)
    stacked = jnp.concatenate([only_head(queries, g) for g in range(3)], axis=0)
    scores = matmul(stacked, keys, NT) + jnp.concatenate([bias] * 3, axis=0)
    highest = jnp.max(scores, axis=1, keepdims=True)
    weights = jnp.exp2(scores - highest).astype(BF16)
    sums = matmul(weights, values)
    scaled = sums * (1.0 / sums[:, 128:129])
    low = lanes((HALF, 128)) < 64
    first = jnp.where(low, scaled[0:HALF, 0:128], scaled[HALF : 2 * HALF, 0:128])
    return first, scaled[2 * HALF : 3 * HALF, 128:256]


def gathered_rows(blocks):
    half = PAIR // 2
    low = lanes((half, 128)) < 64
    parts = [block[0:PAIR] for block in blocks]
    for g in (0, 2):
        even = blocks[g][PAIR:PACKED].astype(F32)
        odd = blocks[g + 1][PAIR:PACKED].astype(F32)
        top = jnp.where(low, even, half_turn(odd))
        bottom = jnp.where(low, half_turn(even), odd)
        parts.append(jnp.concatenate([top, bottom], axis=0).astype(BF16))
    return jnp.concatenate(parts, axis=1)


def kernel(*refs):
    x_hbm, cluster, wq, wk, wv, w_out, out_hbm = refs[:N_ARGS]
    r = types.SimpleNamespace(**dict(zip(SCRATCH, refs[N_ARGS:])))
    s = lax.axis_index("seq")
    h = lax.axis_index("head")
    up, down = lax.rem(h + 1, NH), lax.rem(h + LAST, NH)
    right, left = lax.rem(s + 1, NS), lax.rem(s + NS - 1, NS)
    after = (lax.rem(s + (h + 1) // NH, NS), up)
    before = (lax.rem(s + NS - (LAST - h) // LAST, NS), down)

    barrier = pltpu.get_barrier_semaphore()

    def greet(i, carry):
        pl.semaphore_signal(barrier, 1, device_id=(lax.rem(s + i, NS), h), device_id_type=MESH)
        return carry

    lax.fori_loop(1, NS, greet, 0)
    for t in range(1, NH):
        pl.semaphore_signal(barrier, 1, device_id=(s, lax.rem(h + t, NH)), device_id_type=MESH)
    for near in (before, after):
        pl.semaphore_signal(barrier, 1, device_id=near, device_id_type=MESH)

    x_loads = [
        pltpu.make_async_copy(
            x_hbm.at[pl.ds(p * PAIR, PAIR)], r.x0.at[pl.ds(p * PAIR, PAIR)], r.x_sems.at[p]
        )
        for p in range(NPAIR)
    ]
    w0_loads = window_loads((wq.at[0], wk.at[0], wv.at[0]), r.w0, r.w0_sems)
    w1_loads = [
        pltpu.make_async_copy(src, r.w1.at[pl.ds(start, size)], r.w1_sems.at[i])
        for i, (src, start, size) in enumerate(
            [
                (wk.at[1], 0, 192),
                (wv.at[1, pl.ds(0, 128)], 256, 128),
                (wq.at[1, pl.ds(128, 64)], 384, 64),
                (wv.at[1, pl.ds(128, 64)], 448, 64),
                (wq.at[1, pl.ds(0, 128)], 512, 128),
            ]
        )
    ]
    w2_loads = window_loads((wq.at[2], wk.at[2], wv.at[2]), r.w2.at[h], r.w2_sems)
    wo_loads = [
        pltpu.make_async_copy(
            w_out.at[layer, pl.ds(192 * g + 128 * i, 128 - 64 * i)],
            r.wo.at[layer, pl.ds(128 * g + (512 - 64 * g) * i, 128 - 64 * i)],
            r.wo_sems.at[layer, 2 * g + i],
        )
        for layer in range(3)
        for g in range(NH)
        for i in range(2)
    ]
    for copy in x_loads + w0_loads + w1_loads + wo_loads + w2_loads:
        copy.start()
    r.w1[192:256, :] = jnp.zeros((64, D), BF16)
    for start in (192, 448, 640):
        r.w0[start : start + 64, :] = jnp.zeros((64, D), BF16)

    def clear(g, carry):
        for start in (192, 448, 640):
            r.w2[g, start : start + 64, :] = jnp.zeros((64, D), BF16)
        return carry

    lax.fori_loop(0, NH, clear, 0)
    for copy in x_loads:
        copy.wait()
    pl.semaphore_wait(barrier, NS - 1 + NH - 1 + 2)

    halos = [
        remote(
            r.x0.at[pl.ds(ROWS - HALF, HALF)],
            r.halo0.at[0],
            r.halo0_send.at[0],
            r.halo0_recv.at[0],
            (right, h),
        ),
        remote(
            r.x0.at[pl.ds(0, HALF)], r.halo0.at[1], r.halo0_send.at[1], r.halo0_recv.at[1], (left, h)
        ),
    ]
    for copy in halos:
        copy.start()
    for copy in w0_loads:
        copy.wait()

    def project0(p, carry):
        rows = pl.ds(pl.multiple_of(p * PAIR, PAIR), PAIR)
        projected = matmul(row_normed(r.x0[rows, :]), r.w0[...], NT)
        r.q0[rows, :] = (projected[:, 0:256] * Q_SCALE).astype(BF16)
        inner = pl.ds(pl.multiple_of(p * PAIR + HALF, HALF), PAIR)
        keep_keys(projected[:, 256:768], r.k0.at[inner], r.v0.at[inner])
        return carry

    lax.fori_loop(0, NPAIR, project0, 0)

    def att0_to(p, t):
        block = r.att0.at[h, p]
        peer = (s, lax.rem(h + t, NH))
        return remote(block, block, r.att0_send.at[p, t], r.att0_recv.at[p, t], peer)

    def att0_on(p, t):
        half = PACKED // 2
        block = r.att0.at[lax.rem(h + NH - t, NH), p, pl.ds(half * (t // 2), half)]
        peer = (s, lax.rem(h + t, NH))
        return remote(block, block, r.att0_send.at[p, t - 1], r.att0_recv.at[p, t - 1], peer)

    def attend0(p, carry):
        firsts, thirds = [], []
        for b in range(2):
            begin = pl.multiple_of(p * PAIR + b * HALF, HALF)
            first, third = window_block(
                r.q0[pl.ds(begin, HALF), :],
                r.k0[pl.ds(begin, 3 * HALF), :],
                r.v0[pl.ds(begin, 3 * HALF), :],
                s * ROWS + begin - HALF,
            )
            firsts.append(first)
            thirds.append(third)
        r.att0[h, p, 0:PAIR, :] = jnp.concatenate(firsts, axis=0).astype(BF16)
        r.att0[h, p, PAIR:PACKED, :] = packed_third(jnp.concatenate(thirds, axis=0)).astype(BF16)
        for t in (1, 3):
            att0_to(p, t).start()
        return carry

    lax.fori_loop(1, NPAIR - 1, attend0, 0)
    for copy in halos:
        copy.wait()

    def edge0(side, carry):
        projected = matmul(row_normed(r.halo0[side]), r.w0[256:768, :], NT)
        outer = pl.ds(pl.multiple_of(side * (ROWS + HALF), HALF), HALF)
        keep_keys(projected, r.k0.at[outer], r.v0.at[outer])
        return attend0(side * (NPAIR - 1), carry)

    lax.fori_loop(0, 2, edge0, 0)

    def in_order(i):
        return lax.rem(i + 1, 3) + 2 * (i // 3)

    def hand_on(i):
        p = in_order(i)
        for t in (1, 3):
            att0_to(p, t).wait_recv()
        for t in (1, 3):
            att0_on(p, t).start()

    hand_on(0)

    ids = cluster[...]
    target = ids // 4
    mine = (target == lax.broadcasted_iota(jnp.int32, (NS, ROWS), 0)).astype(F32)
    earlier = (
        lax.broadcasted_iota(jnp.int32, (ROWS, ROWS), 0)
        < lax.broadcasted_iota(jnp.int32, (ROWS, ROWS), 1)
    ).astype(BF16)
    rank = jnp.sum(matmul(mine.astype(BF16), earlier) * mine, axis=0, keepdims=True)
    slot = target * SLOTS + rank.astype(jnp.int32)
    slot_col = jnp.transpose(jnp.broadcast_to(slot.astype(F32), (128, ROWS)))
    r.within[...] = jnp.transpose(
        jnp.broadcast_to((ids - 4 * target).astype(F32), (128, ROWS))
    )
    for p in range(NPAIR):
        col = jnp.concatenate([slot_col[p * PAIR : (p + 1) * PAIR]] * (NS * SLOTS // 128), axis=1)
        r.chosen_back[p * PAIR : (p + 1) * PAIR, :] = (
            col == lanes((PAIR, NS * SLOTS)).astype(F32)
        ).astype(BF16)

    hand_on(1)

    def choose(g, carry):
        rows = lax.broadcasted_iota(jnp.int32, (GROWS, ROWS), 0) + g * GROWS
        r.chosen[pl.ds(pl.multiple_of(g * GROWS, GROWS), GROWS), :] = (rows == slot).astype(BF16)
        return carry

    lax.fori_loop(0, NGROUP, choose, 0)
    hand_on(2)
    for copy in w1_loads + wo_loads:
        copy.wait()

    def finish0(i, carry):
        p = in_order(i)
        for t in (1, 3):
            att0_on(p, t).wait_recv()
        rows = pl.ds(pl.multiple_of(p * PAIR, PAIR), PAIR)
        gathered = gathered_rows([r.att0[g, p] for g in range(NH)])
        total = matmul(gathered, r.wo[0]) + r.x0[rows, :].astype(F32)
        x1 = total.astype(BF16)
        r.x1[rows, :] = x1
        projected = matmul(row_normed(x1), r.w1[...], NT)
        lane = lanes((PAIR, 128))
        mark = (r.within[rows, :] == (lane - 64).astype(F32)).astype(F32)
        scale = jnp.where(lane < 64, Q_SCALE, 1.0)
        r.packed[rows, 0:128] = projected[:, 0:128].astype(BF16)
        r.packed[rows, 128:256] = jnp.where(lane < 64, projected[:, 128:256], mark).astype(BF16)
        r.packed[rows, 256:384] = projected[:, 256:384].astype(BF16)
        r.packed[rows, 384:512] = (projected[:, 384:512] * scale).astype(BF16)
        r.packed[rows, 512:640] = (projected[:, 512:640] * Q_SCALE).astype(BF16)
        return carry

    lax.fori_loop(0, 1, finish0, 0)
    hand_on(3)
    lax.fori_loop(1, NPAIR, finish0, 0)

    def kv_to(k, source):
        return remote(r.out_kv.at[k], r.in_kv.at[source], r.kv_send.at[k], r.kv_recv.at[source], (k, h))

    def q_to(k, source):
        return remote(r.out_q.at[k], r.in_q.at[source], r.q_send.at[k], r.q_recv.at[source], (k, h))

    def answer_to(k, source):
        return remote(r.answer.at[k], r.back.at[source], r.a_send.at[k], r.a_recv.at[source], (k, h))

    my_group = s // GROUP

    def pack(i, carry):
        g = lax.rem(my_group + NGROUP // 2 + i, NGROUP)
        rows = pl.ds(pl.multiple_of(g * GROWS, GROWS), GROWS)
        filled = matmul(r.chosen[rows, :], r.packed[...]).astype(BF16)
        for j in range(GROUP):
            k = g * GROUP + j
            part = filled[j * SLOTS : (j + 1) * SLOTS]
            r.out_kv[k] = part[:, 0:512]
            r.out_q[k] = part[:, 512:640]

            @pl.when(k != s)
            def _():
                kv_to(k, s).start()

            @pl.when(k == s)
            def _():
                r.in_kv[k] = part[:, 0:512]
                r.in_q[k] = part[:, 512:640]

        return carry

    lax.fori_loop(0, NGROUP, pack, 0)

    def send_q(i, carry):
        k = lax.rem(s + NS // 2 + i, NS)

        @pl.when(k != s)
        def _():
            q_to(k, s).start()

        return carry

    lax.fori_loop(0, NS, send_q, 0)

    for copy in w2_loads:
        copy.wait()

    def w2_to(t, i):
        start, size = ((0, 192), (256, 192), (512, 128), (704, 64))[i]
        block = r.w2.at[h, pl.ds(start, size)]
        peer = (s, lax.rem(h + t, NH))
        return remote(block, block, r.w2_send.at[t, i], r.w2_recv.at[t, i], peer)

    w2_copies = [w2_to(t, i) for t in range(1, NH) for i in range(4)]
    for copy in w2_copies:
        copy.start()

    def arrive_kv(k, carry):
        @pl.when(k != s)
        def _():
            kv_to(k, k).wait_recv()

        lane = lanes((SLOTS, 128))
        rows = pl.ds(pl.multiple_of(k * SLOTS, SLOTS), SLOTS)
        tile = r.in_kv[k, :, 128:256].astype(F32)
        other = jnp.where(lane < 68, 1.0 - tile, 0.0)
        r.k_all[rows, 0:128] = r.in_kv[k, :, 0:128]
        r.k_all[rows, 128:256] = jnp.where(lane < 64, tile, other).astype(BF16)
        r.v_all[rows, 0:128] = r.in_kv[k, :, 256:384]
        r.v_all[rows, 128:256] = jnp.where(
            lane < 64, jnp.ones((SLOTS, 128), BF16), r.in_kv[k, :, 384:512]
        )
        return carry

    lax.fori_loop(0, NS, arrive_kv, 0)

    def attend1(i, carry):
        g = lax.rem(my_group + i, NGROUP)
        first = []
        second = []
        for j in range(GROUP):
            k = g * GROUP + j

            @pl.when(k != s)
            def _():
                q_to(k, k).wait_recv()

            first.append(r.in_q[k])
            second.append(
                jnp.where(
                    lanes((SLOTS, 128)) < 64,
                    r.in_kv[k, :, 384:512].astype(F32),
                    FAR * r.in_kv[k, :, 128:256].astype(F32),
                ).astype(BF16)
            )
        queries = jnp.concatenate(
            [jnp.concatenate(first, axis=0), jnp.concatenate(second, axis=0)], axis=1
        )
        scaled = []
        for head in range(3):
            scores = matmul(only_head(queries, head), r.k_all[...], NT)
            highest = jnp.max(scores, axis=1, keepdims=True)
            weights = jnp.exp2(scores - highest).astype(BF16)
            sums = matmul(weights, r.v_all[...])
            scaled.append(sums * (1.0 / sums[:, 128:129]))
        firsts = jnp.where(lanes((GROWS, 128)) < 64, scaled[0][:, 0:128], scaled[1][:, 0:128])
        third = scaled[2][:, 128:256]
        for j in range(GROUP):
            k = g * GROUP + j
            rows = slice(j * SLOTS, (j + 1) * SLOTS)
            a_part = firsts[rows].astype(BF16)
            b_part = packed_third(third[rows]).astype(BF16)
            r.answer[k, 0:SLOTS, :] = a_part
            r.answer[k, SLOTS:ANSWER, :] = b_part

            @pl.when(k != s)
            def _():
                answer_to(k, s).start()

            @pl.when(k == s)
            def _():
                r.back[k, 0:SLOTS, :] = a_part
                r.back[k, SLOTS:ANSWER, :] = b_part

        return carry

    lax.fori_loop(0, NGROUP, attend1, 0)

    def arrive_back(k, carry):
        @pl.when(k != s)
        def _():
            answer_to(k, k).wait_recv()

        start = pl.multiple_of(k * SLOTS, SLOTS)
        r.back_all[pl.ds(start, SLOTS), 0:128] = r.back[k, 0:SLOTS, :]
        third = r.back[k, SLOTS:ANSWER, :]
        turned = half_turn(third.astype(F32)).astype(BF16)
        r.back_all[pl.ds(start, SLOTS), 128:256] = jnp.concatenate([turned, third], axis=0)
        return carry

    lax.fori_loop(0, NS, arrive_back, 0)

    def att1_to(t):
        peer = lax.rem(h + t, NH)
        return remote(r.own1.at[peer], r.att1.at[h], r.att1_send.at[t], r.att1_recv.at[t], (s, peer))

    def att1_from(t):
        source = lax.rem(h + NH - t, NH)
        return remote(
            r.own1.at[source], r.att1.at[source], r.att1_send.at[t], r.att1_recv.at[t], (s, source)
        )

    def unpack(t):
        p = lax.rem(h + t, NH)
        rows = pl.ds(pl.multiple_of(p * PAIR, PAIR), PAIR)
        own = matmul(r.chosen_back[rows, :], r.back_all[...])
        return p, own[:, 0:128].astype(BF16), packed_third(own[:, 128:256]).astype(BF16)

    for t in (2, 1, 3):
        p, first, third = unpack(t)
        r.own1[p, 0:PAIR, :] = first
        r.own1[p, PAIR:PACKED, :] = third
        att1_to(t).start()
    _, first, third = unpack(0)
    r.att1[h, 0:PAIR, :] = first
    r.att1[h, PAIR:PACKED, :] = third
    for t in range(1, NH):
        att1_from(t).wait_recv()
    quarter = pl.ds(pl.multiple_of(h * PAIR, PAIR), PAIR)
    total = matmul(gathered_rows([r.att1[g] for g in range(NH)]), r.wo[1])
    r.x2[...] = (total + r.x1[quarter, :].astype(F32)).astype(BF16)

    halos2 = [
        remote(
            r.x2.at[pl.ds(PAIR - HALF, HALF)],
            r.halo2.at[0],
            r.halo2_send.at[0],
            r.halo2_recv.at[0],
            after,
        ),
        remote(
            r.x2.at[pl.ds(0, HALF)], r.halo2.at[1], r.halo2_send.at[1], r.halo2_recv.at[1], before
        ),
    ]
    for copy in halos2:
        copy.start()
    for copy in w2_copies:
        copy.wait()
    normed = row_normed(r.x2[...])
    inner = pl.ds(HALF, PAIR)
    for g in range(NH):
        projected = matmul(normed, r.w2[g], NT)
        r.q2[g] = (projected[:, 0:256] * Q_SCALE).astype(BF16)
        keep_keys(projected[:, 256:768], r.k2.at[g, inner], r.v2.at[g, inner])
    for copy in halos2:
        copy.wait()
    normed = row_normed(r.halo2[...].reshape(2 * HALF, D))
    for g in range(NH):
        projected = matmul(normed, r.w2[g, 256:768, :], NT)
        for side in range(2):
            outer = pl.ds(side * (PAIR + HALF), HALF)
            keep_keys(
                projected[side * HALF : (side + 1) * HALF], r.k2.at[g, outer], r.v2.at[g, outer]
            )

    def x3_to(b, t):
        block = r.x3.at[pl.ds(pl.multiple_of(h * PAIR + b * HALF, HALF), HALF)]
        peer = (s, lax.rem(h + t, NH))
        return remote(block, block, r.x3_send.at[b, t], r.x3_recv.at[b, t], peer)

    def x3_on(b, t):
        source = lax.rem(h + NH - t, NH)
        half = HALF // 2
        block = r.x3.at[
            pl.ds(pl.multiple_of(source * PAIR + b * HALF + half * (t // 2), half), half)
        ]
        peer = (s, lax.rem(h + t, NH))
        return remote(block, block, r.x3_send.at[b, t - 1], r.x3_recv.at[b, t - 1], peer)

    def write(b, t):
        rows = pl.ds(pl.multiple_of(lax.rem(h + t, NH) * PAIR + b * HALF, HALF), HALF)
        return pltpu.make_async_copy(r.x3.at[rows], out_hbm.at[rows], r.out_sems.at[b, t])

    for b in range(2):
        begin = b * HALF
        firsts, thirds = [], []
        for g in range(NH):
            first, third = window_block(
                r.q2[g, begin : begin + HALF, :],
                r.k2[g, begin : begin + 3 * HALF, :],
                r.v2[g, begin : begin + 3 * HALF, :],
                s * ROWS + h * PAIR + begin - HALF,
            )
            firsts.append(first)
            thirds.append(third)
        low = lanes((HALF, 128)) < 64
        for g in (0, 2):
            firsts.append(jnp.where(low, half_turn(thirds[g]), thirds[g + 1]))
        gathered = jnp.concatenate([first.astype(BF16) for first in firsts], axis=1)
        total = matmul(gathered, r.wo[2]) + r.x2[begin : begin + HALF, :].astype(F32)
        rows = pl.ds(pl.multiple_of(h * PAIR + begin, HALF), HALF)
        r.x3[rows, :] = total.astype(BF16)
        for t in (1, 3):
            x3_to(b, t).start()
        write(b, 0).start()
    for b in range(2):
        for t in (1, 3):
            x3_to(b, t).wait_recv()
        for t in (1, 3):
            x3_on(b, t).start()
        for t in (1, 3):
            write(b, t).start()
    for b in range(2):
        for t in (1, 3):
            x3_on(b, t).wait_recv()
        write(b, 2).start()

    def sent(k, carry):
        @pl.when(k != s)
        def _():
            kv_to(k, s).wait_send()
            q_to(k, s).wait_send()
            answer_to(k, s).wait_send()

        return carry

    lax.fori_loop(0, NS, sent, 0)
    for p in range(NPAIR):
        for t in (1, 3):
            att0_to(p, t).wait_send()
            att0_on(p, t).wait_send()
    for t in range(1, NH):
        att1_to(t).wait_send()
    for b in range(2):
        for t in (1, 3):
            x3_to(b, t).wait_send()
            x3_on(b, t).wait_send()
        for t in range(NH):
            write(b, t).wait()


def shards(tokens, cluster_of, w_query, w_key, w_value, w_out):
    anywhere = pl.BlockSpec(memory_space=pl.ANY)
    return pl.pallas_call(
        kernel,
        out_shape=jax.ShapeDtypeStruct((ROWS, D), BF16),
        in_specs=[anywhere, pl.BlockSpec(memory_space=pltpu.VMEM)] + [anywhere] * 4,
        out_specs=anywhere,
        scratch_shapes=list(SCRATCH.values()),
        compiler_params=pltpu.CompilerParams(
            collective_id=0, has_side_effects=True, vmem_limit_bytes=VMEM_LIMIT
        ),
        name="three_layers",
    )(tokens, cluster_of.reshape(1, ROWS), w_query, w_key, w_value, w_out)


def solution(mesh):
    placed = (
        P("seq", None),
        P("seq"),
        P(None, "head", None),
        P(None, "head", None),
        P(None, "head", None),
        P(),
    )
    return jax.shard_map(
        shards, mesh=mesh, in_specs=placed, out_specs=P("seq", None), check_vma=False
    )
```

profile of v0, /device:TPU:0, one launch (start us, length us, event | category | flops | bytes accessed | tf_op | source)
XLA Modules:
  0.0 133.1 jit_solution(3547986014433311008)
XLA Ops:
  0.0 130.4 %three_layers.1 = bf16[1024,768]{1,0:T(8,128)(2,1)} custom-call(bf16[1024,768]{1,0:T(8,128)(2,1)} %refs_0_.1, s32[1,1024]{1,0:T(1,128)} %bitcast.1, bf16[3,192,768]{2,1,0:T(8,128)(2,1)} %refs_2_.1, bf16[3,192,768]{2,1,0:T(8,128)(2,1)} %refs_3_.1, bf16[3,192,768]{2,1,0:T(8,128)(2,1)} %refs_4_.1, bf16[3,768,768]{2,1,0:T(8,128)(2,1)} %refs_5_.1), custom_call_target="tpu_custom_call" | custom-call | tf_op jit(solution)/shard_map/three_layers/pallas_call | solution.py:676
  130.4 2.7 %copy.8 = bf16[1024,768]{1,0:T(8,128)(2,1)} copy(bf16[1024,768]{1,0:T(8,128)(2,1)} %three_layers.1) | data formatting | bytes 3145728
where the time goes:
time: 133 us
  Pallas kernels  130 us (98%)
  local copies, waits for them, and re-layouts  2.65 us (2%)
    pallas_call x1, Pallas kernels, shards(): pl.pallas_call(kernel, out_shape=jax.ShapeDtypeStruct((ROWS, D), BF16), i...  130 us

commit v1 on v0

--- a/solution.py
+++ b/solution.py
@@ -55,7 +55,8 @@
     return jnp.where(lanes((m, 128)) < 64, half_turn(third[:m]), third[m:])
 
 
-GROUP = 4
+NY, NX, NC = 4, 4, 2
+GROUP = NX
 NGROUP = NS // GROUP
 GROWS = GROUP * SLOTS
 ANSWER = SLOTS + SLOTS // 2
@@ -87,12 +88,17 @@
     "chosen_back": pltpu.VMEM((ROWS, NS * SLOTS), BF16),
     "within": pltpu.VMEM((ROWS, 128), F32),
     "packed": pltpu.VMEM((ROWS, 640), BF16),
-    "out_kv": pltpu.VMEM((NS, SLOTS, 512), BF16),
-    "out_q": pltpu.VMEM((NS, SLOTS, 128), BF16),
-    "in_kv": pltpu.VMEM((NS, SLOTS, 512), BF16),
-    "in_q": pltpu.VMEM((NS, SLOTS, 128), BF16),
-    "k_all": pltpu.VMEM((NS * SLOTS, 256), BF16),
-    "v_all": pltpu.VMEM((NS * SLOTS, 256), BF16),
+    "out_k": pltpu.VMEM((NX, NY, NC, SLOTS, 256), BF16),
+    "out_v": pltpu.VMEM((NY, NX, NC, SLOTS, 256), BF16),
+    "out_q": pltpu.VMEM((NX, NY, NC, SLOTS, 128), BF16),
+    "mid_k": pltpu.VMEM((NY, NC, NX, SLOTS, 256), BF16),
+    "mid_v": pltpu.VMEM((NX, NC, NY, SLOTS, 256), BF16),
+    "mid_q": pltpu.VMEM((NY, NC, NX, SLOTS, 128), BF16),
+    "in_k": pltpu.VMEM((NY, NC, NX, SLOTS, 256), BF16),
+    "in_v": pltpu.VMEM((NY, NC, NX, SLOTS, 256), BF16),
+    "in_q": pltpu.VMEM((NY, NC, NX, SLOTS, 128), BF16),
+    "q_third": pltpu.VMEM((NY, NC, NX, SLOTS, 128), BF16),
+    "scores": pltpu.VMEM((3, GROWS, NS * SLOTS), F32),
     "answer": pltpu.VMEM((NS, ANSWER, 128), BF16),
     "back": pltpu.VMEM((NS, ANSWER, 128), BF16),
     "back_all": pltpu.VMEM((NS * SLOTS, 256), BF16),
@@ -111,10 +117,18 @@
     "att0_recv": DMA((NPAIR, NH)),
     "att1_send": DMA((NH,)),
     "att1_recv": DMA((NH,)),
-    "kv_send": DMA((NS,)),
-    "kv_recv": DMA((NS,)),
-    "q_send": DMA((NS,)),
-    "q_recv": DMA((NS,)),
+    "k1_send": DMA((NX,)),
+    "k1_recv": DMA((NX,)),
+    "v1_send": DMA((NY,)),
+    "v1_recv": DMA((NY,)),
+    "q1_send": DMA((NX,)),
+    "q1_recv": DMA((NX,)),
+    "k2_send": DMA((NY, NC)),
+    "k2_recv": DMA((NY, NC)),
+    "v2_send": DMA((NX, NC)),
+    "v2_recv": DMA((NX, NC)),
+    "q2_send": DMA((NY, NC)),
+    "q2_recv": DMA((NY, NC)),
     "a_send": DMA((NS,)),
     "a_recv": DMA((NS,)),
     "x3_send": DMA((2, NH)),
@@ -389,50 +403,114 @@
     hand_on(3)
     lax.fori_loop(1, NPAIR, finish0, 0)
 
-    def kv_to(k, source):
-        return remote(r.out_kv.at[k], r.in_kv.at[source], r.kv_send.at[k], r.kv_recv.at[source], (k, h))
-
-    def q_to(k, source):
-        return remote(r.out_q.at[k], r.in_q.at[source], r.q_send.at[k], r.q_recv.at[source], (k, h))
+    y, x, c = s // (NX * NC), lax.rem(s // NC, NX), lax.rem(s, NC)
+
+    def device(y_at, x_at, c_at):
+        return (lax.rem(y_at, NY) * (NX * NC) + lax.rem(x_at, NX) * NC + lax.rem(c_at, NC), h)
+
+    def along_x(out, mid, send, recv, d):
+        column = lax.rem(x + d, NX)
+        return remote(out.at[column], mid.at[:, :, x], send.at[d], recv.at[d], device(y, x + d, c))
+
+    def along_y(out, mid, send, recv, d):
+        row = lax.rem(y + d, NY)
+        return remote(out.at[row], mid.at[:, :, y], send.at[d], recv.at[d], device(y + d, x, c))
+
+    def k1(d):
+        return along_x(r.out_k, r.mid_k, r.k1_send, r.k1_recv, d)
+
+    def q1(d):
+        return along_x(r.out_q, r.mid_q, r.q1_send, r.q1_recv, d)
+
+    def v1(d):
+        return along_y(r.out_v, r.mid_v, r.v1_send, r.v1_recv, d)
+
+    def then_y(mid, into, send, recv, d, e):
+        block = mid.at[lax.rem(y + d, NY), lax.rem(c + e, NC)]
+        peer = device(y + d, x, c + e)
+        return remote(block, into.at[y, c], send.at[d, e], recv.at[d, e], peer)
+
+    def k2(d, e):
+        return then_y(r.mid_k, r.in_k, r.k2_send, r.k2_recv, d, e)
+
+    def q2(d, e):
+        return then_y(r.mid_q, r.in_q, r.q2_send, r.q2_recv, d, e)
+
+    def v2(d, e):
+        block = r.mid_v.at[lax.rem(x + d, NX), lax.rem(c + e, NC)]
+        peer = device(y, x + d, c + e)
+        return remote(block, r.in_v.at[:, c, x], r.v2_send.at[d, e], r.v2_recv.at[d, e], peer)
 
     def answer_to(k, source):
         return remote(r.answer.at[k], r.back.at[source], r.a_send.at[k], r.a_recv.at[source], (k, h))
 
-    my_group = s // GROUP
+    def column_rows(column):
+        return jnp.concatenate(
+            [
+                r.chosen[
+                    pl.ds(pl.multiple_of((NX * n + column) * NC * SLOTS, NC * SLOTS), NC * SLOTS), :
+                ]
+                for n in range(NY)
+            ],
+            axis=0,
+        )
 
     def pack(i, carry):
-        g = lax.rem(my_group + NGROUP // 2 + i, NGROUP)
-        rows = pl.ds(pl.multiple_of(g * GROWS, GROWS), GROWS)
-        filled = matmul(r.chosen[rows, :], r.packed[...]).astype(BF16)
-        for j in range(GROUP):
-            k = g * GROUP + j
-            part = filled[j * SLOTS : (j + 1) * SLOTS]
-            r.out_kv[k] = part[:, 0:512]
-            r.out_q[k] = part[:, 512:640]
-
-            @pl.when(k != s)
-            def _():
-                kv_to(k, s).start()
-
-            @pl.when(k == s)
-            def _():
-                r.in_kv[k] = part[:, 0:512]
-                r.in_q[k] = part[:, 512:640]
-
-        return carry
-
-    lax.fori_loop(0, NGROUP, pack, 0)
-
-    def send_q(i, carry):
-        k = lax.rem(s + NS // 2 + i, NS)
-
-        @pl.when(k != s)
+        d = lax.rem(i + 2, NX)
+        column, row = lax.rem(x + d, NX), lax.rem(y + d, NY)
+        keys = matmul(column_rows(column), r.packed[:, 0:256])
+        lane = lanes(keys.shape)
+        keys = jnp.where(lane < 192, keys, jnp.where(lane < 192 + 4, 1.0 - keys, 0.0))
+        keys = keys.astype(BF16).reshape(NY, NC, SLOTS, 256)
+        size = NX * NC * SLOTS
+        rows = pl.ds(pl.multiple_of(row * size, size), size)
+        values = matmul(r.chosen[rows, :], r.packed[:, 256:512])
+        values = values.astype(BF16).reshape(NX, NC, SLOTS, 256)
+
+        @pl.when(d != 0)
         def _():
-            q_to(k, s).start()
-
-        return carry
-
-    lax.fori_loop(0, NS, send_q, 0)
+            r.out_k[column] = keys
+            k1(d).start()
+            r.out_v[row] = values
+            v1(d).start()
+
+        @pl.when(d == 0)
+        def _():
+            for n in range(NY):
+                for e in range(NC):
+                    r.mid_k[n, e, x] = keys[n, e]
+                    r.mid_v[n, e, y] = values[n, e]
+
+        return carry
+
+    lax.fori_loop(0, NX, pack, 0)
+
+    def pack_q(i, carry):
+        d = lax.rem(i + 2, NX)
+        column = lax.rem(x + d, NX)
+        queries = matmul(column_rows(column), r.packed[:, 512:640])
+        queries = queries.astype(BF16).reshape(NY, NC, SLOTS, 128)
+
+        @pl.when(d != 0)
+        def _():
+            r.out_q[column] = queries
+            q1(d).start()
+
+        @pl.when(d == 0)
+        def _():
+            for n in range(NY):
+                for e in range(NC):
+                    r.mid_q[n, e, x] = queries[n, e]
+
+        return carry
+
+    lax.fori_loop(0, NX, pack_q, 0)
+    others = [(d, e) for d in (2, 1, 3, 0) for e in range(NC) if (d, e) != (0, 0)]
+    for first, then in ((k1, k2), (v1, v2), (q1, q2)):
+        for d in (1, 2, 3):
+            first(d).wait_recv()
+        for d, e in others:
+            then(d, e).start()
 
     for copy in w2_loads:
         copy.wait()
@@ -447,58 +525,57 @@
     for copy in w2_copies:
         copy.start()
 
-    def arrive_kv(k, carry):
-        @pl.when(k != s)
-        def _():
-            kv_to(k, k).wait_recv()
-
-        lane = lanes((SLOTS, 128))
-        rows = pl.ds(pl.multiple_of(k * SLOTS, SLOTS), SLOTS)
-        tile = r.in_kv[k, :, 128:256].astype(F32)
-        other = jnp.where(lane < 68, 1.0 - tile, 0.0)
-        r.k_all[rows, 0:128] = r.in_kv[k, :, 0:128]
-        r.k_all[rows, 128:256] = jnp.where(lane < 64, tile, other).astype(BF16)
-        r.v_all[rows, 0:128] = r.in_kv[k, :, 256:384]
-        r.v_all[rows, 128:256] = jnp.where(
-            lane < 64, jnp.ones((SLOTS, 128), BF16), r.in_kv[k, :, 384:512]
+    r.in_k[y, c] = r.mid_k[y, c]
+    r.in_q[y, c] = r.mid_q[y, c]
+    for n in range(NY):
+        r.in_v[n, c, x] = r.mid_v[x, c, n]
+    for then in (k2, v2, q2):
+        for d, e in others:
+            then(d, e).wait_recv()
+
+    def settle(g, carry):
+        at = (g // NC, lax.rem(g, NC))
+        lane = lax.broadcasted_iota(jnp.int32, (NX, SLOTS, 128), 2)
+        other = r.in_k[(*at, slice(None), slice(None), slice(128, 256))].astype(F32)
+        third = r.in_v[(*at, slice(None), slice(None), slice(128, 256))]
+        marks = jnp.where(lane < 68, FAR * (1.0 - other), 0.0)
+        r.q_third[at] = jnp.where(lane < 64, third.astype(F32), marks).astype(BF16)
+        r.in_v[(*at, slice(None), slice(None), slice(128, 256))] = jnp.where(
+            lane < 64, jnp.ones_like(third), third
         )
         return carry
 
-    lax.fori_loop(0, NS, arrive_kv, 0)
+    lax.fori_loop(0, NGROUP, settle, 0)
+    my_group = y * NC + c
+
+    def score(i, head):
+        g = lax.rem(my_group + i, NGROUP)
+        at = (g // NC, lax.rem(g, NC))
+        queries = jnp.concatenate(
+            [r.in_q[at].reshape(GROWS, 128), r.q_third[at].reshape(GROWS, 128)], axis=1
+        )
+        keys = r.in_k[...].reshape(NS * SLOTS, 256)
+        r.scores[head] = matmul(only_head(queries, head), keys, NT)
+
+    def weigh(head):
+        scores = r.scores[head]
+        highest = jnp.max(scores, axis=1, keepdims=True)
+        weights = jnp.exp2(scores - highest).astype(BF16)
+        sums = matmul(weights, r.in_v[...].reshape(NS * SLOTS, 256))
+        return sums * (1.0 / sums[:, 128:129])
+
+    score(0, 0)
 
     def attend1(i, carry):
         g = lax.rem(my_group + i, NGROUP)
-        first = []
-        second = []
-        for j in range(GROUP):
-            k = g * GROUP + j
-
-            @pl.when(k != s)
-            def _():
-                q_to(k, k).wait_recv()
-
-            first.append(r.in_q[k])
-            second.append(
-                jnp.where(
-                    lanes((SLOTS, 128)) < 64,
-                    r.in_kv[k, :, 384:512].astype(F32),
-                    FAR * r.in_kv[k, :, 128:256].astype(F32),
-                ).astype(BF16)
-            )
-        queries = jnp.concatenate(
-            [jnp.concatenate(first, axis=0), jnp.concatenate(second, axis=0)], axis=1
-        )
         scaled = []
         for head in range(3):
-            scores = matmul(only_head(queries, head), r.k_all[...], NT)
-            highest = jnp.max(scores, axis=1, keepdims=True)
-            weights = jnp.exp2(scores - highest).astype(BF16)
-            sums = matmul(weights, r.v_all[...])
-            scaled.append(sums * (1.0 / sums[:, 128:129]))
+            score(i + (head + 1) // 3, (head + 1) % 3)
+            scaled.append(weigh(head))
         firsts = jnp.where(lanes((GROWS, 128)) < 64, scaled[0][:, 0:128], scaled[1][:, 0:128])
         third = scaled[2][:, 128:256]
         for j in range(GROUP):
-            k = g * GROUP + j
+            k = (g // NC) * (NX * NC) + j * NC + lax.rem(g, NC)
             rows = slice(j * SLOTS, (j + 1) * SLOTS)
             a_part = firsts[rows].astype(BF16)
             b_part = packed_third(third[rows]).astype(BF16)
@@ -650,13 +727,17 @@
     def sent(k, carry):
         @pl.when(k != s)
         def _():
-            kv_to(k, s).wait_send()
-            q_to(k, s).wait_send()
             answer_to(k, s).wait_send()
 
         return carry
 
     lax.fori_loop(0, NS, sent, 0)
+    for d in (1, 2, 3):
+        for first in (k1, v1, q1):
+            first(d).wait_send()
+    for d, e in others:
+        for then in (k2, v2, q2):
+            then(d, e).wait_send()
     for p in range(NPAIR):
         for t in (1, 3):
             att0_to(p, t).wait_send()

time: 133 us -> 128 us (0.962)
  Pallas kernels: 130 us -> 126 us
    pallas_call x1, Pallas kernels: 130 us -> 126 us  [shards(): pl.pallas_call(kernel, out_shape=jax.ShapeDtypeStruct((ROWS, D), BF16), i...]
where the time goes in v1:
time: 128 us
  Pallas kernels  126 us (98%)
  local copies, waits for them, and re-layouts  2.65 us (2%)
    pallas_call x1, Pallas kernels, shards(): pl.pallas_call(kernel, out_shape=jax.ShapeDtypeStruct((ROWS, D), BF16), i...  126 us
    unnamed x1, local copies, waits for them, and re-layouts  2.65 us

profile of v1, /device:TPU:0, one launch (start us, length us, event | category | flops | bytes accessed | tf_op | source)
XLA Modules:
  0.0 128.3 jit_solution(208115483704514326)
XLA Ops:
  0.0 125.6 %three_layers.1 = bf16[1024,768]{1,0:T(8,128)(2,1)} custom-call(bf16[1024,768]{1,0:T(8,128)(2,1)} %refs_0_.1, s32[1,1024]{1,0:T(1,128)} %bitcast.1, bf16[3,192,768]{2,1,0:T(8,128)(2,1)} %refs_2_.1, bf16[3,192,768]{2,1,0:T(8,128)(2,1)} %refs_3_.1, bf16[3,192,768]{2,1,0:T(8,128)(2,1)} %refs_4_.1, bf16[3,768,768]{2,1,0:T(8,128)(2,1)} %refs_5_.1), custom_call_target="tpu_custom_call" | custom-call | tf_op jit(solution)/shard_map/three_layers/pallas_call | solution.py:757
  125.7 2.7 %copy.8 = bf16[1024,768]{1,0:T(8,128)(2,1)} copy(bf16[1024,768]{1,0:T(8,128)(2,1)} %three_layers.1) | data formatting | bytes 3145728

commit v2 on v1

--- a/solution.py
+++ b/solution.py
@@ -106,8 +106,10 @@
     "w0_sems": DMA((4,)),
     "w1_sems": DMA((5,)),
     "w2_sems": DMA((4,)),
-    "w2_send": DMA((NH, 4)),
-    "w2_recv": DMA((NH, 4)),
+    "w2_send": DMA((NH, 3)),
+    "w2_recv": DMA((NH, 3)),
+    "w2_on_send": DMA((NH, 3)),
+    "w2_on_recv": DMA((NH, 3)),
     "wo_sems": DMA((3, 2 * NH)),
     "halo0_send": DMA((2,)),
     "halo0_recv": DMA((2,)),
@@ -252,7 +254,7 @@
         for g in range(NH)
         for i in range(2)
     ]
-    for copy in x_loads + w0_loads + w1_loads + wo_loads + w2_loads:
+    for copy in x_loads + w0_loads:
         copy.start()
     r.w1[192:256, :] = jnp.zeros((64, D), BF16)
     for start in (192, 448, 640):
@@ -284,6 +286,8 @@
         copy.start()
     for copy in w0_loads:
         copy.wait()
+    for copy in w1_loads + wo_loads + w2_loads:
+        copy.start()
 
     def project0(p, carry):
         rows = pl.ds(pl.multiple_of(p * PAIR, PAIR), PAIR)
@@ -485,6 +489,26 @@
 
     lax.fori_loop(0, NX, pack, 0)
 
+    for copy in w2_loads:
+        copy.wait()
+    pieces = ((512 * c, 128), (128 + 576 * c, 64), (256 + 96 * c, 96))
+    twin = device(y, x, c + 1)
+
+    def w2_to(t, i):
+        start, size = pieces[i]
+        block = r.w2.at[h, pl.ds(pl.multiple_of(start, 32), size)]
+        peer = (s, lax.rem(h + t, NH))
+        return remote(block, block, r.w2_send.at[t, i], r.w2_recv.at[t, i], peer)
+
+    def w2_on(t, i):
+        start, size = pieces[i]
+        block = r.w2.at[lax.rem(h + NH - t, NH), pl.ds(pl.multiple_of(start, 32), size)]
+        return remote(block, block, r.w2_on_send.at[t, i], r.w2_on_recv.at[t, i], twin)
+
+    halves = [(t, i) for t in (2, 1, 3) for i in range(3)]
+    for t, i in halves:
+        w2_to(t, i).start()
+
     def pack_q(i, carry):
         d = lax.rem(i + 2, NX)
         column = lax.rem(x + d, NX)
@@ -494,7 +518,6 @@
         @pl.when(d != 0)
         def _():
             r.out_q[column] = queries
-            q1(d).start()
 
         @pl.when(d == 0)
         def _():
@@ -506,32 +529,24 @@
 
     lax.fori_loop(0, NX, pack_q, 0)
     others = [(d, e) for d in (2, 1, 3, 0) for e in range(NC) if (d, e) != (0, 0)]
-    for first, then in ((k1, k2), (v1, v2), (q1, q2)):
+    for first, then in ((k1, k2), (v1, v2)):
         for d in (1, 2, 3):
             first(d).wait_recv()
         for d, e in others:
             then(d, e).start()
 
-    for copy in w2_loads:
-        copy.wait()
-
-    def w2_to(t, i):
-        start, size = ((0, 192), (256, 192), (512, 128), (704, 64))[i]
-        block = r.w2.at[h, pl.ds(start, size)]
-        peer = (s, lax.rem(h + t, NH))
-        return remote(block, block, r.w2_send.at[t, i], r.w2_recv.at[t, i], peer)
-
-    w2_copies = [w2_to(t, i) for t in range(1, NH) for i in range(4)]
-    for copy in w2_copies:
-        copy.start()
-
+    for d in (2, 1, 3):
+        q1(d).start()
     r.in_k[y, c] = r.mid_k[y, c]
-    r.in_q[y, c] = r.mid_q[y, c]
     for n in range(NY):
         r.in_v[n, c, x] = r.mid_v[x, c, n]
-    for then in (k2, v2, q2):
+    for then in (k2, v2):
         for d, e in others:
             then(d, e).wait_recv()
+
+    for t, i in halves:
+        w2_to(t, i).wait_recv()
+        w2_on(t, i).start()
 
     def settle(g, carry):
         at = (g // NC, lax.rem(g, NC))
@@ -546,10 +561,17 @@
         return carry
 
     lax.fori_loop(0, NGROUP, settle, 0)
-    my_group = y * NC + c
+    for d in (1, 2, 3):
+        q1(d).wait_recv()
+    for d, e in ((0, 1), (3, 0), (3, 1), (2, 0), (2, 1), (1, 0), (1, 1)):
+        q2(d, e).start()
+    r.in_q[y, c] = r.mid_q[y, c]
+
+    def group(i):
+        return lax.rem(y + i // NC, NY) * NC + lax.rem(c + i, NC)
 
     def score(i, head):
-        g = lax.rem(my_group + i, NGROUP)
+        g = group(i)
         at = (g // NC, lax.rem(g, NC))
         queries = jnp.concatenate(
             [r.in_q[at].reshape(GROWS, 128), r.q_third[at].reshape(GROWS, 128)], axis=1
@@ -566,11 +588,14 @@
 
     score(0, 0)
 
-    def attend1(i, carry):
-        g = lax.rem(my_group + i, NGROUP)
+    def attend1(i, carry, last=False):
+        g = group(i)
+        if not last:
+            q2(lax.rem(NY - (i + 1) // NC, NY), lax.rem(i + 1, NC)).wait_recv()
         scaled = []
         for head in range(3):
-            score(i + (head + 1) // 3, (head + 1) % 3)
+            if not (last and head == 2):
+                score(i + (head + 1) // 3, (head + 1) % 3)
             scaled.append(weigh(head))
         firsts = jnp.where(lanes((GROWS, 128)) < 64, scaled[0][:, 0:128], scaled[1][:, 0:128])
         third = scaled[2][:, 128:256]
@@ -593,21 +618,27 @@
 
         return carry
 
-    lax.fori_loop(0, NGROUP, attend1, 0)
-
-    def arrive_back(k, carry):
-        @pl.when(k != s)
-        def _():
-            answer_to(k, k).wait_recv()
-
-        start = pl.multiple_of(k * SLOTS, SLOTS)
-        r.back_all[pl.ds(start, SLOTS), 0:128] = r.back[k, 0:SLOTS, :]
-        third = r.back[k, SLOTS:ANSWER, :]
-        turned = half_turn(third.astype(F32)).astype(BF16)
-        r.back_all[pl.ds(start, SLOTS), 128:256] = jnp.concatenate([turned, third], axis=0)
-        return carry
-
-    lax.fori_loop(0, NS, arrive_back, 0)
+    lax.fori_loop(0, NGROUP - 1, attend1, 0)
+    attend1(NGROUP - 1, 0, last=True)
+
+    def arrive_back(g, carry):
+        for j in range(4):
+            k = 4 * g + j
+
+            @pl.when(k != s)
+            def _():
+                answer_to(k, k).wait_recv()
+
+        block = r.back[pl.ds(4 * g, 4)]
+        rows = pl.ds(pl.multiple_of(g * PAIR, PAIR), PAIR)
+        third = block[:, SLOTS:ANSWER, :]
+        turned = half_turn(third.astype(F32).reshape(HALF, 128)).astype(BF16)
+        turned = turned.reshape(4, SLOTS // 2, 128)
+        r.back_all[rows, 0:128] = block[:, 0:SLOTS, :].reshape(PAIR, 128)
+        r.back_all[rows, 128:256] = jnp.concatenate([turned, third], axis=1).reshape(PAIR, 128)
+        return carry
+
+    lax.fori_loop(0, NS // 4, arrive_back, 0)
 
     def att1_to(t):
         peer = lax.rem(h + t, NH)
@@ -653,8 +684,8 @@
     ]
     for copy in halos2:
         copy.start()
-    for copy in w2_copies:
-        copy.wait()
+    for t, i in halves:
+        w2_on(t, i).wait_recv()
     normed = row_normed(r.x2[...])
     inner = pl.ds(HALF, PAIR)
     for g in range(NH):
@@ -732,6 +763,9 @@
         return carry
 
     lax.fori_loop(0, NS, sent, 0)
+    for t, i in halves:
+        w2_to(t, i).wait_send()
+        w2_on(t, i).wait_send()
     for d in (1, 2, 3):
         for first in (k1, v1, q1):
             first(d).wait_send()

time: 128 us -> 127 us (level); the launches traced: 128 us -> 126 us
  Pallas kernels: 126 us -> 123 us
    pallas_call x1, Pallas kernels: 126 us -> 123 us  [shards(): pl.pallas_call(kernel, out_shape=jax.ShapeDtypeStruct((ROWS, D), BF16), i...]
where the time goes in v2:
time: 127 us; the launch traced here: 126 us
  Pallas kernels  123 us (97%)
  local copies, waits for them, and re-layouts  2.65 us (2%)
    pallas_call x1, Pallas kernels, shards(): pl.pallas_call(kernel, out_shape=jax.ShapeDtypeStruct((ROWS, D), BF16), i...  123 us
    unnamed x1, local copies, waits for them, and re-layouts  2.65 us

profile of v2, /device:TPU:0, one launch (start us, length us, event | category | flops | bytes accessed | tf_op | source)
XLA Modules:
  0.0 125.9 jit_solution(9453031197736604450)
XLA Ops:
  0.0 123.2 %three_layers.1 = bf16[1024,768]{1,0:T(8,128)(2,1)} custom-call(bf16[1024,768]{1,0:T(8,128)(2,1)} %refs_0_.1, s32[1,1024]{1,0:T(1,128)} %bitcast.1, bf16[3,192,768]{2,1,0:T(8,128)(2,1)} %refs_2_.1, bf16[3,192,768]{2,1,0:T(8,128)(2,1)} %refs_3_.1, bf16[3,192,768]{2,1,0:T(8,128)(2,1)} %refs_4_.1, bf16[3,768,768]{2,1,0:T(8,128)(2,1)} %refs_5_.1), custom_call_target="tpu_custom_call" | custom-call | tf_op jit(solution)/shard_map/three_layers/pallas_call | solution.py:791
  123.2 2.7 %copy.8 = bf16[1024,768]{1,0:T(8,128)(2,1)} copy(bf16[1024,768]{1,0:T(8,128)(2,1)} %three_layers.1) | data formatting | bytes 3145728

commit v3 on v2

--- a/solution.py
+++ b/solution.py
@@ -692,16 +692,13 @@
         projected = matmul(normed, r.w2[g], NT)
         r.q2[g] = (projected[:, 0:256] * Q_SCALE).astype(BF16)
         keep_keys(projected[:, 256:768], r.k2.at[g, inner], r.v2.at[g, inner])
-    for copy in halos2:
-        copy.wait()
-    normed = row_normed(r.halo2[...].reshape(2 * HALF, D))
-    for g in range(NH):
-        projected = matmul(normed, r.w2[g, 256:768, :], NT)
-        for side in range(2):
-            outer = pl.ds(side * (PAIR + HALF), HALF)
-            keep_keys(
-                projected[side * HALF : (side + 1) * HALF], r.k2.at[g, outer], r.v2.at[g, outer]
-            )
+    def edge2(side):
+        halos2[side].wait()
+        normed = row_normed(r.halo2[side])
+        outer = pl.ds(side * (PAIR + HALF), HALF)
+        for g in range(NH):
+            projected = matmul(normed, r.w2[g, 256:768, :], NT)
+            keep_keys(projected, r.k2.at[g, outer], r.v2.at[g, outer])
 
     def x3_to(b, t):
         block = r.x3.at[pl.ds(pl.multiple_of(h * PAIR + b * HALF, HALF), HALF)]
@@ -722,6 +719,7 @@
         return pltpu.make_async_copy(r.x3.at[rows], out_hbm.at[rows], r.out_sems.at[b, t])
 
     for b in range(2):
+        edge2(b)
         begin = b * HALF
         firsts, thirds = [], []
         for g in range(NH):

time: 127 us -> 126 us (level)
  no operation moved by 1% of the time
where the time goes in v3:
time: 126 us; the launch traced here: 125 us
  Pallas kernels  122 us (97%)
  local copies, waits for them, and re-layouts  2.65 us (2%)
    pallas_call x1, Pallas kernels, shards(): pl.pallas_call(kernel, out_shape=jax.ShapeDtypeStruct((ROWS, D), BF16), i...  122 us
    unnamed x1, local copies, waits for them, and re-layouts  2.65 us

profile of v3, /device:TPU:0, one launch (start us, length us, event | category | flops | bytes accessed | tf_op | source)
XLA Modules:
  0.0 125.1 jit_solution(9771591906382700013)
XLA Ops:
  0.0 122.4 %three_layers.1 = bf16[1024,768]{1,0:T(8,128)(2,1)} custom-call(bf16[1024,768]{1,0:T(8,128)(2,1)} %refs_0_.1, s32[1,1024]{1,0:T(1,128)} %bitcast.1, bf16[3,192,768]{2,1,0:T(8,128)(2,1)} %refs_2_.1, bf16[3,192,768]{2,1,0:T(8,128)(2,1)} %refs_3_.1, bf16[3,192,768]{2,1,0:T(8,128)(2,1)} %refs_4_.1, bf16[3,768,768]{2,1,0:T(8,128)(2,1)} %refs_5_.1), custom_call_target="tpu_custom_call" | custom-call | tf_op jit(solution)/shard_map/three_layers/pallas_call | solution.py:789
  122.4 2.7 %copy.8 = bf16[1024,768]{1,0:T(8,128)(2,1)} copy(bf16[1024,768]{1,0:T(8,128)(2,1)} %three_layers.1) | data formatting | bytes 3145728
